TPU v7x, 256 devices: a whole 4x4x8 slice. The times are simulated.
256 devices in a mesh: leaf: 32 (over x_lo, z, core), launch: 8 (over y, x_hi).
Axes of the slice: x: 4 (x_hi: 2, x_lo: 2; x = x_hi * 2 + x_lo), y: 4, z: 8, core: 2. Of those that a mesh axis runs over, the one named last changes fastest.
Arguments:
- right_side: bfloat16 [4, 128, 128, 1024], P(None, 'leaf', None, 'launch'), may hold values from -6 to 6
- diag_inverse: bfloat16 [4, 128, 128, 128], P(None, 'leaf'), may hold values from -0.5 to 0.5
- factors: bfloat16 [6, 128, 16, 128, 128], P(None, 'leaf', 'launch'), may hold values from -0.078125 to 0.078125
- pattern: int32 [6, 128, 16], P(None, 'leaf'), may hold values from 0 to 127
- owner_map: int32 [3, 128], replicated, may hold values from 0 to 127, each once within a row
Outputs:
- solutions: bfloat16 [4, 128, 128, 1024], P(None, 'leaf', None, 'launch')
Inputs may be any that keep to these rules, and one draw needn't show every extreme that they name: `pattern`: entries name tree supernodes of the pair's lower level; one descendant may appear more than once. `owner_map`: each row is a permutation of the slots of one of the levels 0 to 2.
All inputs are finite; a program needn't handle non-finite values.
Results may differ from a plain program's by a relative error of at most 0.008.
Values may be sent and summed in bfloat16 or wider, within the bound.
A program may use at most 128 MiB of HBM per device.

v0:
```python
import jax
import jax.numpy as jnp
from jax import lax
from jax.sharding import PartitionSpec as P

LEVELS = 4


def solve_level(inverse_blocks, rhs_blocks, updates):
    residue = (rhs_blocks.astype(jnp.float32) - updates).astype(jnp.bfloat16)
    solved = jnp.einsum("sij,sjc->sic", inverse_blocks, residue, preferred_element_type=jnp.float32)
    return solved.astype(jnp.bfloat16)


def per_device(right_side, diag_inverse, factors, pattern, owner_map):
    owned_blocks = right_side.shape[1]
    block_rows = right_side.shape[2]
    column_shard = right_side.shape[3]
    pending = [
        jnp.zeros((owned_blocks, block_rows, column_shard), jnp.float32) for height in range(LEVELS)
    ]
    solutions = []
    for height in range(LEVELS):
        if height == 0:
            updates = jnp.zeros((owned_blocks, block_rows, column_shard), jnp.float32)
        else:
            updates = pending[height]
        own_solve = solve_level(diag_inverse[height], right_side[height], updates)
        solutions.append(own_solve)
        if height + 1 < LEVELS:
            first_pair = height * (2 * LEVELS - height - 1) // 2
            above_count = LEVELS - height - 1
            gathered = lax.all_gather(own_solve, "leaf", axis=0, tiled=True)
            slot_map = jnp.take(
                owner_map[height], pattern[first_pair : first_pair + above_count], axis=0
            )
            picked = gathered[slot_map]
            products = jnp.einsum(
                "usqij,usqjc->usic",
                lax.all_gather(
                    factors[first_pair : first_pair + above_count], "launch", axis=2, tiled=True
                ),
                picked,
                preferred_element_type=jnp.float32,
            )
            for offset in range(above_count):
                pending[height + 1 + offset] = pending[height + 1 + offset] + products[offset]
    return jnp.stack(solutions)


def solution(mesh):
    return jax.shard_map(
        per_device,
        mesh=mesh,
        in_specs=(
            P(None, "leaf", None, "launch"),
            P(None, "leaf", None, None),
            P(None, "leaf", "launch", None, None),
            P(None, "leaf", None),
            P(),
        ),
        out_specs=P(None, "leaf", None, "launch"),
        check_vma=False,
    )
```

profile of v0, /device:TPU:1, one launch (start us, length us, event | category | flops | bytes accessed | tf_op | source)
XLA Modules:
  0.0 472.4 jit_solution(11981084951245167463)
XLA Ops:
  6.5 1.8 convolution_convert_fusion.3
  8.4 2.1 slice.71
  11.4 0.8 slice_bitcast_fusion
  12.2 1.5 gather_fusion
  14.2 66.1 %all-gather.7.cloned.1.call-done = bf16[128,128,128]{2,1,0:T(8,128)(2,1)} async-done(((bf16[4,128,128]{2,1,0:T(8,128)(2,1)}), bf16[128,128,128]{2,1,0:T(8,128)(2,1)}) %all-gather.7.cloned.1.call-update) | async-done | bytes 4194320 | tf_op jit(solution)/shard_map/all_gather | solution.py:33
  80.3 10.2 %gather_fusion.1 = bf16[192,128,128]{2,1,0:T(8,128)(2,1)} fusion(bf16[128,128,128]{2,1,0:T(8,128)(2,1)} %all-gather.7.cloned.1.call-done, s32[1024]{0:T(1024)S(1)} %pad_clamp_fusion.4), kind=kCustom, calls=%fused_computation.1 | custom fusion | bytes 12583680 | tf_op jit(solution)/shard_map/gather | solution.py:37
  90.4 85.2 %all-gather.9.cloned.1.call-done = bf16[3,4,16,128,128]{4,3,2,1,0:T(8,128)(2,1)} async-done(((bf16[3,4,2,128,128]{4,3,2,1,0:T(8,128)(2,1)}), bf16[3,4,16,128,128]{4,3,2,1,0:T(8,128)(2,1)}) %all-gather.9.cloned.1.call-update) | async-done | bytes 6291472 | tf_op jit(solution)/shard_map/all_gather | solution.py:40
  175.7 6.7 %convolution_bitcast_fusion = f32[3,4,128,128]{2,3,1,0:T(8,128)S(1)} fusion(bf16[3,4,16,128,128]{4,3,2,1,0:T(8,128)(2,1)} %bitcast.97, bf16[3,4,16,128,128]{4,3,2,1,0:T(8,128)(2,1)} %all-gather.9.cloned.1.call-done), kind=kOutput, calls=%fused_computation.8 | convolution fusion | flops 805306368 | bytes 13369344 | tf_op jit(solution)/shard_map/usqij,usqjc->usic/dot_general | solution.py:38
  182.3 1.8 convolution_convert_fusion.2
  184.2 0.8 slice.78
  185.2 1.2 gather_fusion.2
  186.8 63.1 %all-gather.11.cloned.1.call-done = bf16[128,128,128]{2,1,0:T(8,128)(2,1)} async-done(((bf16[4,128,128]{2,1,0:T(8,128)(2,1)}), bf16[128,128,128]{2,1,0:T(8,128)(2,1)}) %all-gather.11.cloned.1.call-update) | async-done | bytes 4194320 | tf_op jit(solution)/shard_map/all_gather | solution.py:33
  249.8 5.2 %gather_fusion.3 = bf16[128,128,128]{2,1,0:T(8,128)(2,1)} fusion(bf16[128,128,128]{2,1,0:T(8,128)(2,1)} %all-gather.11.cloned.1.call-done, s32[1024]{0:T(1024)S(1)} %pad_clamp_fusion.2), kind=kCustom, calls=%fused_computation.3 | custom fusion | bytes 8389120 | tf_op jit(solution)/shard_map/gather | solution.py:37
  255.1 72.5 %all-gather.13.cloned.1.call-done = bf16[2,4,16,128,128]{4,3,2,1,0:T(8,128)(2,1)} async-done(((bf16[2,4,2,128,128]{4,3,2,1,0:T(8,128)(2,1)}), bf16[2,4,16,128,128]{4,3,2,1,0:T(8,128)(2,1)}) %all-gather.13.cloned.1.call-update) | async-done | bytes 4194320 | tf_op jit(solution)/shard_map/all_gather | solution.py:40
  327.6 4.9 %convolution_bitcast_fusion.1 = f32[2,4,128,128]{2,3,1,0:T(8,128)S(1)} fusion(bf16[2,4,16,128,128]{4,3,2,1,0:T(8,128)(2,1)} %bitcast.98, bf16[2,4,16,128,128]{4,3,2,1,0:T(8,128)(2,1)} %all-gather.13.cloned.1.call-done), kind=kOutput, calls=%fused_computation.9 | convolution fusion | flops 536870912 | bytes 8912896 | tf_op jit(solution)/shard_map/usqij,usqjc->usic/dot_general | solution.py:38
  332.5 1.8 convolution_convert_fusion.1
  334.3 0.7 slice.86
  335.2 0.8 gather_fusion.4
  336.1 0.8 copy.42
  336.9 63.1 %all-gather.15.cloned.1.call-done = bf16[128,128,128]{2,1,0:T(8,128)(2,1)} async-done(((bf16[4,128,128]{2,1,0:T(8,128)(2,1)}), bf16[128,128,128]{2,1,0:T(8,128)(2,1)}) %all-gather.15.cloned.1.call-update) | async-done | bytes 4194320 | tf_op jit(solution)/shard_map/all_gather | solution.py:33
  400.0 3.1 gather_fusion.5
  403.1 57.2 %all-gather.17.cloned.1.call-done = bf16[1,4,16,128,128]{4,3,2,1,0:T(8,128)(2,1)} async-done(((bf16[1,4,2,128,128]{4,3,2,1,0:T(8,128)(2,1)}), bf16[1,4,16,128,128]{4,3,2,1,0:T(8,128)(2,1)}) %all-gather.17.cloned.1.call-update) | async-done | bytes 2097168 | tf_op jit(solution)/shard_map/all_gather | solution.py:40
  460.4 3.3 fusion.16
  463.6 1.9 pad_maximum_fusion
  (44 shorter events, 2.2 us)
Async XLA Ops:
  6.5 73.7 %all-gather.7.cloned.1.call-start = ((), (), s32[]{:S(2)}) async-start(), calls=%async_computation | async-start | bytes 4325376 | tf_op jit(solution)/shard_map/all_gather | solution.py:33
  8.4 5.5 %copy-start.3 = (s32[6,4,16]{2,1,0:T(4,128)S(1)}, s32[6,4,16]{2,1,0:T(4,128)}, u32[]{:S(2)}) copy-start(s32[6,4,16]{2,1,0:T(4,128)} %param.8) | copy-start | bytes 4612
  8.4 5.6 %copy-start.2 = (bf16[4,4,128,128]{3,2,1,0:T(8,128)(2,1)S(1)}, bf16[4,4,128,128]{3,2,1,0:T(8,128)(2,1)}, u32[]{:S(2)}) copy-start(bf16[4,4,128,128]{3,2,1,0:T(8,128)(2,1)} %param.5) | copy-start | bytes 1572868
  8.4 167.3 %all-gather.9.cloned.1.call-start = ((), (), s32[]{:S(2)}) async-start(), calls=%async_computation.1 | async-start | bytes 7077888 | tf_op jit(solution)/shard_map/all_gather | solution.py:40
  10.6 239.2 %all-gather.11.cloned.1.call-start = ((), (), s32[]{:S(2)}) async-start(), calls=%async_computation.2 | async-start | bytes 4325376 | tf_op jit(solution)/shard_map/all_gather | solution.py:33
  175.7 8.5 %copy-start = (bf16[6,4,2,128,128]{4,3,2,1,0:T(8,128)(2,1)S(1)}, bf16[6,4,2,128,128]{4,3,2,1,0:T(8,128)(2,1)}, u32[]{:S(2)}) copy-start(bf16[6,4,2,128,128]{4,3,2,1,0:T(8,128)(2,1)} %param.7) | copy-start | bytes 4718596
  184.1 143.5 %all-gather.13.cloned.1.call-start = ((), (), s32[]{:S(2)}) async-start(), calls=%async_computation.3 | async-start | bytes 4718592 | tf_op jit(solution)/shard_map/all_gather | solution.py:40
  185.0 214.9 %all-gather.15.cloned.1.call-start = ((), (), s32[]{:S(2)}) async-start(), calls=%async_computation.4 | async-start | bytes 4325376 | tf_op jit(solution)/shard_map/all_gather | solution.py:33
  334.3 126.1 %all-gather.17.cloned.1.call-start = ((), (), s32[]{:S(2)}) async-start(), calls=%async_computation.5 | async-start | bytes 2359296 | tf_op jit(solution)/shard_map/all_gather | solution.py:40
  336.9 126.7 %copy-start.1 = (bf16[4,128,128]{2,1,0:T(8,128)(2,1)S(1)}, bf16[4,128,128]{2,1,0:T(8,128)(2,1)}, u32[]{:S(2)}) copy-start(bf16[4,128,128]{2,1,0:T(8,128)(2,1)} %convolution_convert_fusion.3) | copy-start | bytes 393220
Sparse Core Ops, SparseCore 0:
  9.2 71.0 all-gather.6
  82.9 92.7 all-gather.8
  184.3 65.5 all-gather.10
  252.3 75.2 all-gather.12
  334.4 65.5 all-gather.14
  402.4 57.8 all-gather.16
where the time goes:
time: 473 us; the launch traced here: 472 us
  waiting for transfers between devices  407 us (86%)
  local copies, waits for them, and re-layouts  28.5 us (6%)
  matrix products  20.1 us (4%)
  between operations  13.6 us (3%)
    all_gather x3, waiting for transfers between devices, per_device(): lax.all_gather(factors[first_pair:first_pair + above_count], 'launch', ax...  215 us
    all_gather x3, waiting for transfers between devices, per_device(): gathered = lax.all_gather(own_solve, 'leaf', axis=0, tiled=True)  192 us
    gather x3, local copies, waits for them, and re-layouts, per_device(): picked = gathered[slot_map]  18.6 us
    dot_general x2, matrix products, per_device(): jnp.einsum('usqij,usqjc->usic', lax.all_gather(factors[first_pair:first_p...  11.5 us
  transfers between devices with their start and end apart: 6, of which 6 were waited for; matrix products, arithmetic and copies ran while one was open for 6% of the time, Pallas kernels for 0%

commit v1 on v0

v1 whole, which is shorter than its diff:
```python
import jax
import jax.numpy as jnp
from jax import lax
from jax.experimental import pallas as pl
from jax.experimental.pallas import tpu as pltpu
from jax.sharding import PartitionSpec as P

LEVELS = 4
FAN = 16
SUPS = 128
OWN = 4
BLK = 128
COLS = 128
PARTS = 2
CHUNK = COLS // PARTS
PAIRS = 6
ZS = 8
YS = 4
LEAFS = 16

PAIR_ORDER = (0, 1, 3, 2, 4, 5)
X_FIRST = (2, 2, 2, 3, 2, 3)

GATHER_SEMS = 33
FACTOR_SEMS = 15
MESH = pl.DeviceIdType.MESH


def pair_of(lower, upper):
    return lower * (2 * LEVELS - lower - 1) // 2 + upper - lower - 1


def transposed_product(rows, blocks):
    return lax.dot_general(rows, blocks, (((1,), (1,)), ((), ())), preferred_element_type=jnp.float32)


def kernel(*refs):
    pattern, owner, right_side, diag, own_factors, out = refs[:6]
    solved = refs[6 : 6 + 3 * PARTS]
    (factors, pending, rhs_t, last, g_send, g_recv, f_send, f_recv, own_sem) = refs[6 + 3 * PARTS :]

    leaf = lax.axis_index("leaf")
    launch = lax.axis_index("launch")
    core, z, x_lo = leaf % 2, (leaf // 2) % ZS, leaf // LEAFS
    y, x_hi = launch // 2, launch % 2

    def leaf_at(xl, zz, k):
        return xl * LEAFS + zz * 2 + k

    def z_at(step):
        return (z + step + ZS) % ZS

    def y_at(step):
        return (y + step + YS) % YS

    z_up = (leaf_at(x_lo, z_at(1), core), launch)
    z_down = (leaf_at(x_lo, z_at(-1), core), launch)
    x_near = (leaf_at(1 - x_lo, z, core), launch)
    sibling = (leaf_at(x_lo, z, 1 - core), launch)
    x_far = (leaf, y * 2 + (1 - x_hi))
    y_up = (leaf, y_at(1) * 2 + x_hi)
    y_down = (leaf, y_at(-1) * 2 + x_hi)
    partners = (z_up, z_down, x_near, sibling, x_far, y_up, y_down)

    sends = []

    def send(src, dst, send_sem, recv_sem, device):
        copy = pltpu.make_async_remote_copy(
            src_ref=src, dst_ref=dst, send_sem=send_sem, recv_sem=recv_sem, device_id=device, device_id_type=MESH
        )
        copy.start()
        sends.append(copy)

    def arrived(dst, recv_sem, send_sem):
        pltpu.make_async_remote_copy(
            src_ref=dst, dst_ref=dst, send_sem=send_sem, recv_sem=recv_sem, device_id=sibling, device_id_type=MESH
        ).wait_recv()

    def slots(u, xl, zz, k, half=None):
        first = leaf_at(xl, zz, k) * OWN
        if half is None:
            return solved[u].at[pl.ds(first, OWN)]
        return solved[u].at[pl.ds(first + half * (OWN // 2), OWN // 2)]

    def g_put(u, ref, at, device):
        send(ref, ref, g_send.at[u, at], g_recv.at[u, at], device)

    def g_wait(u, ref, at):
        arrived(ref, g_recv.at[u, at], g_send.at[u, at])

    columns = (x_lo, 1 - x_lo)

    def ring(stream, down, step):
        return 1 + stream * 8 + down * 4 + step - 1

    def side(stream, offset):
        return 17 + stream * 8 + offset % ZS

    def spread(u, stream):
        block = slots(u, columns[stream], z, core)
        g_put(u, block, ring(stream, 0, 1), z_up)
        g_put(u, block, ring(stream, 1, 1), z_down)
        g_put(u, block, side(stream, 0), sibling)

    def gather_start(u):
        g_put(u, slots(u, x_lo, z, core), 0, x_near)
        spread(u, 0)

    def gather_step(u, step):
        if step == 0:
            g_wait(u, slots(u, 1 - x_lo, z, core), 0)
            spread(u, 1)
            return
        for stream in range(2):
            xl = columns[stream]
            if step < 4:
                for down, device in ((0, z_up), (1, z_down)):
                    offset = step if down else -step
                    block = slots(u, xl, z_at(offset), core)
                    g_wait(u, block, ring(stream, down, step))
                    onward = block if step < 3 else slots(u, xl, z_at(offset), core, down)
                    g_put(u, onward, ring(stream, down, step + 1), device)
                    g_put(u, block, side(stream, offset), sibling)
            else:
                for down in range(2):
                    g_wait(u, slots(u, xl, z_at(4), core, down), ring(stream, down, 4))
                g_put(u, slots(u, xl, z_at(4), core), side(stream, 4), sibling)

    def gather_end(u):
        for stream in range(2):
            for offset in range(ZS):
                g_wait(u, slots(u, columns[stream], z_at(offset), 1 - core), side(stream, offset))

    def held(p, yy, xh, y_first, half=None):
        cut = X_FIRST[p]
        which = pl.ds(cut, OWN - cut) if y_first else pl.ds(0, cut)
        if half is None:
            return factors.at[p, yy * 2 + xh, which]
        return factors.at[p, yy * 2 + xh, which, pl.ds(half, 1)]

    def f_put(p, src, dst, at, device):
        send(src, dst, f_send.at[p, at], f_recv.at[p, at], device)

    def f_wait(p, ref, at):
        arrived(ref, f_recv.at[p, at], f_send.at[p, at])

    def own_copy(p):
        return pltpu.make_async_copy(own_factors.at[p], factors.at[p, launch], own_sem.at[p])

    def factors_send(p):
        cut = X_FIRST[p]
        src_x, src_y = own_factors.at[p, pl.ds(0, cut)], own_factors.at[p, pl.ds(cut, OWN - cut)]
        dst_x, dst_y = held(p, y, x_hi, False), held(p, y, x_hi, True)
        f_put(p, src_x, dst_x, 0, x_far)
        f_put(p, src_x, dst_x, 1, y_up)
        f_put(p, src_x, dst_x, 2, y_down)
        f_put(p, src_y, dst_y, 7, y_up)
        f_put(p, src_y, dst_y, 8, y_down)
        f_put(p, src_y, dst_y, 11, x_far)
        own_copy(p).start()

    def factors_second(p):
        far = held(p, y, 1 - x_hi, False)
        f_wait(p, far, 0)
        f_put(p, far, far, 3, y_up)
        f_put(p, far, far, 4, y_down)
        below, above = held(p, y_at(-1), x_hi, True), held(p, y_at(1), x_hi, True)
        f_wait(p, below, 7)
        half = held(p, y_at(-1), x_hi, True, 0)
        f_put(p, half, half, 9, y_up)
        f_put(p, below, below, 12, x_far)
        f_wait(p, above, 8)
        half = held(p, y_at(1), x_hi, True, 1)
        f_put(p, half, half, 10, y_down)
        f_put(p, above, above, 13, x_far)

    def factors_third(p):
        below = held(p, y_at(-1), x_hi, False)
        f_wait(p, below, 1)
        f_put(p, below, below, 5, y_up)
        above = held(p, y_at(1), 1 - x_hi, False)
        f_wait(p, above, 4)
        f_put(p, above, above, 6, y_down)
        for half in range(2):
            f_wait(p, held(p, y_at(2), x_hi, True, half), 9 + half)
        opposite = held(p, y_at(2), x_hi, True)
        f_put(p, opposite, opposite, 14, x_far)

    def factors_end(p):
        f_wait(p, held(p, y_at(1), x_hi, False), 2)
        f_wait(p, held(p, y_at(-1), 1 - x_hi, False), 3)
        f_wait(p, held(p, y_at(2), x_hi, False), 5)
        f_wait(p, held(p, y_at(2), 1 - x_hi, False), 6)
        for at, step in ((11, 0), (12, -1), (13, 1), (14, 2)):
            f_wait(p, held(p, y_at(step), 1 - x_hi, True), at)
        own_copy(p).wait()

    def unit(level, part):
        return level * PARTS + part

    def update(lower, upper, part, a):
        p, source = pair_of(lower, upper), solved[unit(lower, part)]
        total = jnp.zeros((CHUNK, BLK), jnp.float32)
        for group in range(FAN // 2):
            picked = [source[owner[lower, pattern[p, a, group * 2 + q]]] for q in range(2)]
            blocks = [factors[p, group, a, q] for q in range(2)]
            total += transposed_product(jnp.concatenate(picked, axis=1), jnp.concatenate(blocks, axis=1))
        return total

    def later(lower, upper, part):
        def body(a, _):
            product = update(lower, upper, part, a)
            if lower > 0:
                product += pending[upper, part, a]
            pending[upper, part, a] = product
            return 0

        lax.fori_loop(0, OWN, body, 0)

    def solve(level, part):
        def body(a, _):
            residue = rhs_t[level, a, pl.ds(part * CHUNK, CHUNK)]
            if level > 0:
                updates = update(level - 1, level, part, a)
                if level > 1:
                    updates += pending[level, part, a]
                residue = (residue.astype(jnp.float32) - updates).astype(jnp.bfloat16)
            result = transposed_product(residue, diag[level, a]).astype(jnp.bfloat16)
            if level < LEVELS - 1:
                solved[unit(level, part)][leaf * OWN + a] = result
            else:
                last[a, pl.ds(part * CHUNK, CHUNK)] = result
            return 0

        lax.fori_loop(0, OWN, body, 0)

    def turn(level):
        for a in range(OWN):
            rhs_t[level, a] = right_side[level, a].T

    def write(level):
        for a in range(OWN):
            if level < LEVELS - 1:
                parts = [solved[unit(level, part)][leaf * OWN + a] for part in range(PARTS)]
                block = jnp.concatenate(parts, axis=0)
            else:
                block = last[a]
            out[level, a] = block.T

    barrier = pltpu.get_barrier_semaphore()
    for device in partners:
        pl.semaphore_signal(barrier, inc=1, device_id=device, device_id_type=MESH)
    turn(0)
    solve(0, 0)
    solve(0, 1)
    pl.semaphore_wait(barrier, len(partners))

    PER, LAG, EVERY, SECOND, THIRD = 7, 3, 4, 3, 6
    done = set()

    def need(p):
        if p not in done:
            done.add(p)
            factors_end(p)

    def chain(part, at):
        if at < 0 or at >= 3 * PER:
            return
        level, step = divmod(at, PER)
        u = unit(level, part)
        if step == 0:
            if level > 0:
                need(pair_of(level - 1, level))
                solve(level, part)
            gather_start(u)
        elif step <= 5:
            gather_step(u, step - 1)
            if step == 3 and level == 1:
                need(pair_of(0, 2))
                later(0, 2, part)
            if step == 5 and level == 2:
                need(pair_of(0, 3))
                later(0, 3, part)
        else:
            gather_end(u)

    for tick in range(3 * PER + LAG + 8):
        for i, p in enumerate(PAIR_ORDER):
            if tick == EVERY * i + SECOND:
                factors_second(p)
            if tick == EVERY * i + THIRD:
                factors_third(p)
        chain(0, tick)
        for i, p in enumerate(PAIR_ORDER):
            if tick == EVERY * i:
                factors_send(p)
        chain(1, tick - LAG)
        if tick == 4:
            for level in range(1, LEVELS):
                turn(level)
    need(pair_of(1, 3))
    for part in range(PARTS):
        later(1, 3, part)
    for level in range(LEVELS - 1):
        write(level)
    need(pair_of(2, 3))
    for part in range(PARTS):
        solve(3, part)
    write(3)
    for copy in sends:
        copy.wait_send()


def per_device(right_side, diag_inverse, factors, pattern, owner_map):
    vmem = pl.BlockSpec(memory_space=pltpu.VMEM)
    smem = pl.BlockSpec(memory_space=pltpu.SMEM)
    return pl.pallas_call(
        kernel,
        out_shape=jax.ShapeDtypeStruct(right_side.shape, jnp.bfloat16),
        in_specs=[smem, smem, vmem, vmem, pl.BlockSpec(memory_space=pl.ANY)],
        out_specs=vmem,
        scratch_shapes=[pltpu.VMEM((SUPS, CHUNK, BLK), jnp.bfloat16)] * (3 * PARTS)
        + [
            pltpu.VMEM((PAIRS, FAN // 2, OWN, 2, BLK, BLK), jnp.bfloat16),
            pltpu.VMEM((LEVELS, PARTS, OWN, CHUNK, BLK), jnp.float32),
            pltpu.VMEM((LEVELS, OWN, COLS, BLK), jnp.bfloat16),
            pltpu.VMEM((OWN, COLS, BLK), jnp.bfloat16),
            pltpu.SemaphoreType.DMA((3 * PARTS, GATHER_SEMS)),
            pltpu.SemaphoreType.DMA((3 * PARTS, GATHER_SEMS)),
            pltpu.SemaphoreType.DMA((PAIRS, FACTOR_SEMS)),
            pltpu.SemaphoreType.DMA((PAIRS, FACTOR_SEMS)),
            pltpu.SemaphoreType.DMA((PAIRS,)),
        ],
        compiler_params=pltpu.CompilerParams(collective_id=0, has_side_effects=True, vmem_limit_bytes=48 << 20),
        name="substitution",
    )(pattern, owner_map, right_side, diag_inverse, factors)


def solution(mesh):
    return jax.shard_map(
        per_device,
        mesh=mesh,
        in_specs=(
            P(None, "leaf", None, "launch"),
            P(None, "leaf", None, None),
            P(None, "leaf", "launch", None, None),
            P(None, "leaf", None),
            P(),
        ),
        out_specs=P(None, "leaf", None, "launch"),
        check_vma=False,
    )
```

time: 473 us -> 134 us (0.28)
  the two profiles are of different devices: /device:TPU:1 before, /device:TPU:16 now
where the time goes in v1:
time: 134 us
  Pallas kernels  128 us (96%)
  local copies, waits for them, and re-layouts  5.67 us (4%)
    pallas_call x1, Pallas kernels, per_device(): pl.pallas_call(kernel, out_shape=jax.ShapeDtypeStruct(right_side.shape, j...  128 us
    unnamed x11, local copies, waits for them, and re-layouts  5.67 us

profile of v1, /device:TPU:16, one launch (start us, length us, event | category | flops | bytes accessed | tf_op | source)
XLA Modules:
  0.0 133.5 jit_solution(2566148926900659483)
XLA Ops:
  0.0 0.0 copy-start
  0.0 1.4 %copy-done = bf16[6,4,2,128,128]{4,3,2,1,0:T(8,128)(2,1)S(1)} copy-done((bf16[6,4,2,128,128]{4,3,2,1,0:T(8,128)(2,1)S(1)}, bf16[6,4,2,128,128]{4,3,2,1,0:T(8,128)(2,1)}, u32[]{:S(2)}) %copy-start) | copy-done | bytes 1572888
  1.4 0.0 copy-start.1
  1.4 1.0 copy-done.1
  2.5 0.0 copy-start.2
  2.5 1.0 copy-done.2
  3.5 0.0 copy-start.3
  3.5 0.7 copy-done.3
  4.2 0.0 copy-start.4
  4.2 0.7 copy-done.4
  4.9 127.8 %substitution.1 = bf16[4,4,128,128]{3,2,1,0:T(8,128)(2,1)S(1)} custom-call(s32[6,4,16]{2,1,0:T(4,128)S(1)} %copy-done.3, s32[3,128]{1,0:T(4,128)S(1)} %copy-done.4, bf16[4,4,128,128]{3,2,1,0:T(8,128)(2,1)S(1)} %copy-done.1, bf16[4,4,128,128]{3,2,1,0:T(8,128)(2,1)S(1)} %copy-done.2, bf16[6,4,2,128,128]{4,3,2,1,0:T(8,128)(2,1)S(1)} %copy-done), custom_call_target="tpu_custom_call" | custom-call | tf_op jit(solution)/shard_map/substitution/pallas_call | solution.py:317
  132.7 0.8 copy.7
Async XLA Ops:
  0.0 1.4 %copy-start = (bf16[6,4,2,128,128]{4,3,2,1,0:T(8,128)(2,1)S(1)}, bf16[6,4,2,128,128]{4,3,2,1,0:T(8,128)(2,1)}, u32[]{:S(2)}) copy-start(bf16[6,4,2,128,128]{4,3,2,1,0:T(8,128)(2,1)} %refs_4_.1) | copy-start | bytes 4718596
  1.4 1.0 copy-start.1
  2.5 1.0 copy-start.2
  3.5 0.7 copy-start.3
  4.2 0.7 copy-start.4

commit v2 on v1

--- a/solution.py
+++ b/solution.py
@@ -18,8 +18,28 @@
 YS = 4
 LEAFS = 16
 
-PAIR_ORDER = (0, 1, 3, 2, 4, 5)
-X_FIRST = (2, 2, 2, 3, 2, 3)
+X_FIRST = (2, 2, 3, 3, 3, 2)
+
+STEPS = (
+    (5,0,2), (0,0,0), (5,1,2), (0,0,1), (5,0,0), (5,3,2), (1,0,0), (5,0,1), (5,3,0), (7,0,1), (7,0,0), (2,0,1,0,0,1),
+    (2,0,0,0,1,1), (5,0,3), (2,0,0,0,0,1), (5,3,1), (2,0,0,1,0,1), (2,0,0,1,1,1), (1,0,1), (5,4,3), (2,0,1,0,1,1),
+    (2,0,0,0,0,2), (2,0,0,1,0,2), (2,0,1,1,0,1), (9,0), (6,0), (5,4,1), (2,0,0,1,1,2), (2,0,1,1,1,1), (2,0,0,0,1,2),
+    (2,0,1,0,1,2), (2,0,0,1,1,3), (8,0,0), (7,3,0), (2,0,0,0,0,3), (2,0,1,1,0,2), (8,0,1), (2,0,1,1,1,2),
+    (2,0,0,1,0,3), (5,1,1), (2,0,1,0,0,2), (5,2,0), (7,3,1), (2,0,0,0,1,3), (2,0,1,1,1,3), (2,0,1,1,0,3), (3,0,0,0),
+    (5,4,2), (2,0,1,0,0,3), (3,0,0,1), (6,3), (5,5,2), (5,2,2), (2,0,1,0,1,3), (0,1,0), (5,1,0), (3,0,1,1), (3,0,1,0),
+    (0,1,1), (2,1,0,0,0,1), (1,1,0), (2,1,0,0,1,1), (5,4,0), (7,1,1), (2,1,1,0,1,1), (1,1,1), (2,1,1,0,0,1), (5,5,1),
+    (2,1,0,1,0,1), (5,1,3), (6,1), (2,1,0,1,1,1), (7,1,0), (2,1,1,1,0,1), (8,3,1), (2,1,1,0,0,2), (2,1,1,1,1,1),
+    (2,1,0,0,1,2), (2,1,0,1,1,2), (8,3,0), (2,1,0,1,0,2), (9,3), (2,1,1,1,0,2), (2,1,1,0,1,2), (9,1), (8,1,1),
+    (2,1,0,0,0,2), (2,1,1,0,0,3), (7,4,0), (2,1,1,1,1,2), (5,3,3), (5,5,0), (8,1,0), (2,1,0,1,1,3), (2,1,0,0,1,3),
+    (6,2), (7,4,1), (2,1,0,1,0,3), (5,2,1), (2,1,1,1,0,3), (6,4), (2,1,0,0,0,3), (2,1,1,0,1,3), (3,1,0,1),
+    (2,1,1,1,1,3), (4,0,2,1), (3,1,0,0), (4,0,2,0), (3,1,1,0), (0,2,0), (5,2,3), (3,1,1,1), (0,2,1), (7,2,0), (1,2,0),
+    (7,5,0), (2,2,0,0,0,1), (2,2,0,0,1,1), (7,2,1), (6,5), (7,5,1), (8,2,1), (1,2,1), (2,2,1,0,0,1), (8,2,0),
+    (2,2,1,0,1,1), (9,4), (2,2,0,1,0,1), (8,4,1), (2,2,0,0,1,2), (2,2,1,1,0,1), (2,2,1,1,1,1), (2,2,0,1,1,1),
+    (2,2,1,0,0,2), (2,2,1,0,1,2), (9,2), (9,5), (2,2,0,1,0,2), (8,4,0), (2,2,1,1,0,2), (2,2,1,1,1,2), (5,5,3),
+    (2,2,0,0,0,2), (8,5,1), (2,2,0,1,1,2), (2,2,1,0,1,3), (2,2,1,0,0,3), (8,5,0), (4,0,3,0), (2,2,1,1,0,3),
+    (2,2,1,1,1,3), (2,2,0,0,1,3), (2,2,0,1,0,3), (4,0,3,1), (2,2,0,1,1,3), (2,2,0,0,0,3), (4,1,3,0), (3,2,1,0),
+    (3,2,1,1), (4,1,3,1), (3,2,0,1), (3,2,0,0), (0,3,1), (0,3,0),
+)
 
 GATHER_SEMS = 33
 FACTOR_SEMS = 15
@@ -35,9 +55,11 @@
 
 
 def kernel(*refs):
-    pattern, owner, right_side, diag, own_factors, out = refs[:6]
+    pattern_in, owner_in, right_side_in, diag_in, own_factors, out = refs[:6]
     solved = refs[6 : 6 + 3 * PARTS]
-    (factors, pending, rhs_t, last, g_send, g_recv, f_send, f_recv, own_sem) = refs[6 + 3 * PARTS :]
+    (factors, pending, rhs_t, last, pattern, owner, right_side, diag, g_send, g_recv, f_send, f_recv, own_sem, in_sem) = (
+        refs[6 + 3 * PARTS :]
+    )
 
     leaf = lax.axis_index("leaf")
     launch = lax.axis_index("launch")
@@ -106,25 +128,23 @@
         g_put(u, slots(u, x_lo, z, core), 0, x_near)
         spread(u, 0)
 
-    def gather_step(u, step):
-        if step == 0:
-            g_wait(u, slots(u, 1 - x_lo, z, core), 0)
-            spread(u, 1)
-            return
-        for stream in range(2):
-            xl = columns[stream]
-            if step < 4:
-                for down, device in ((0, z_up), (1, z_down)):
-                    offset = step if down else -step
-                    block = slots(u, xl, z_at(offset), core)
-                    g_wait(u, block, ring(stream, down, step))
-                    onward = block if step < 3 else slots(u, xl, z_at(offset), core, down)
-                    g_put(u, onward, ring(stream, down, step + 1), device)
-                    g_put(u, block, side(stream, offset), sibling)
-            else:
-                for down in range(2):
-                    g_wait(u, slots(u, xl, z_at(4), core, down), ring(stream, down, 4))
-                g_put(u, slots(u, xl, z_at(4), core), side(stream, 4), sibling)
+    def gather_near(u):
+        g_wait(u, slots(u, 1 - x_lo, z, core), 0)
+        spread(u, 1)
+
+    def gather_ring(u, stream, down, hop):
+        xl, offset = columns[stream], hop if down else -hop
+        block = slots(u, xl, z_at(offset), core)
+        g_wait(u, block, ring(stream, down, hop))
+        onward = block if hop < 3 else slots(u, xl, z_at(offset), core, down)
+        g_put(u, onward, ring(stream, down, hop + 1), z_down if down else z_up)
+        g_put(u, block, side(stream, offset), sibling)
+
+    def gather_last(u, stream):
+        xl = columns[stream]
+        for down in range(2):
+            g_wait(u, slots(u, xl, z_at(4), core, down), ring(stream, down, 4))
+        g_put(u, slots(u, xl, z_at(4), core), side(stream, 4), sibling)
 
     def gather_end(u):
         for stream in range(2):
@@ -147,40 +167,42 @@
     def own_copy(p):
         return pltpu.make_async_copy(own_factors.at[p], factors.at[p, launch], own_sem.at[p])
 
-    def factors_send(p):
+    def factors_send(p, stage):
         cut = X_FIRST[p]
         src_x, src_y = own_factors.at[p, pl.ds(0, cut)], own_factors.at[p, pl.ds(cut, OWN - cut)]
         dst_x, dst_y = held(p, y, x_hi, False), held(p, y, x_hi, True)
-        f_put(p, src_x, dst_x, 0, x_far)
-        f_put(p, src_x, dst_x, 1, y_up)
-        f_put(p, src_x, dst_x, 2, y_down)
-        f_put(p, src_y, dst_y, 7, y_up)
-        f_put(p, src_y, dst_y, 8, y_down)
-        f_put(p, src_y, dst_y, 11, x_far)
-        own_copy(p).start()
-
-    def factors_second(p):
+        if stage == 0:
+            f_put(p, src_x, dst_x, 0, x_far)
+            own_copy(p).start()
+        elif stage == 1:
+            f_put(p, src_x, dst_x, 1, y_up)
+            f_put(p, src_x, dst_x, 2, y_down)
+        elif stage == 2:
+            f_put(p, src_y, dst_y, 7, y_up)
+            f_put(p, src_y, dst_y, 8, y_down)
+        else:
+            f_put(p, src_y, dst_y, 11, x_far)
+
+    def factors_far(p):
         far = held(p, y, 1 - x_hi, False)
         f_wait(p, far, 0)
         f_put(p, far, far, 3, y_up)
         f_put(p, far, far, 4, y_down)
-        below, above = held(p, y_at(-1), x_hi, True), held(p, y_at(1), x_hi, True)
-        f_wait(p, below, 7)
-        half = held(p, y_at(-1), x_hi, True, 0)
-        f_put(p, half, half, 9, y_up)
-        f_put(p, below, below, 12, x_far)
-        f_wait(p, above, 8)
-        half = held(p, y_at(1), x_hi, True, 1)
-        f_put(p, half, half, 10, y_down)
-        f_put(p, above, above, 13, x_far)
-
-    def factors_third(p):
-        below = held(p, y_at(-1), x_hi, False)
-        f_wait(p, below, 1)
-        f_put(p, below, below, 5, y_up)
-        above = held(p, y_at(1), 1 - x_hi, False)
-        f_wait(p, above, 4)
-        f_put(p, above, above, 6, y_down)
+
+    def factors_onward(p, down):
+        step = 1 if down else -1
+        block = held(p, y_at(step), x_hi, True)
+        f_wait(p, block, 7 + down)
+        half = held(p, y_at(step), x_hi, True, down)
+        f_put(p, half, half, 9 + down, y_down if down else y_up)
+        f_put(p, block, block, 12 + down, x_far)
+
+    def factors_around(p, down):
+        block = held(p, y_at(1), 1 - x_hi, False) if down else held(p, y_at(-1), x_hi, False)
+        f_wait(p, block, 4 if down else 1)
+        f_put(p, block, block, 5 + down, y_down if down else y_up)
+
+    def factors_last(p):
         for half in range(2):
             f_wait(p, held(p, y_at(2), x_hi, True, half), 9 + half)
         opposite = held(p, y_at(2), x_hi, True)
@@ -215,7 +237,7 @@
             pending[upper, part, a] = product
             return 0
 
-        lax.fori_loop(0, OWN, body, 0)
+        lax.fori_loop(0, OWN, body, 0, unroll=True)
 
     def solve(level, part):
         def body(a, _):
@@ -232,7 +254,7 @@
                 last[a, pl.ds(part * CHUNK, CHUNK)] = result
             return 0
 
-        lax.fori_loop(0, OWN, body, 0)
+        lax.fori_loop(0, OWN, body, 0, unroll=True)
 
     def turn(level):
         for a in range(OWN):
@@ -250,74 +272,83 @@
     barrier = pltpu.get_barrier_semaphore()
     for device in partners:
         pl.semaphore_signal(barrier, inc=1, device_id=device, device_id_type=MESH)
+    loads = [
+        pltpu.make_async_copy(src.at[part], dst.at[part], in_sem.at[at, part])
+        for part in range(LEVELS)
+        for at, (src, dst) in enumerate(((right_side_in, right_side), (diag_in, diag)))
+    ]
+    tables = [
+        pltpu.make_async_copy(src, dst, in_sem.at[2, at])
+        for at, (src, dst) in enumerate(((pattern_in, pattern), (owner_in, owner)))
+    ]
+    for copy in loads + tables:
+        copy.start()
+    for copy in loads[:2]:
+        copy.wait()
     turn(0)
-    solve(0, 0)
-    solve(0, 1)
+    for part in range(PARTS):
+        solve(0, part)
     pl.semaphore_wait(barrier, len(partners))
 
-    PER, LAG, EVERY, SECOND, THIRD = 7, 3, 4, 3, 6
-    done = set()
-
-    def need(p):
-        if p not in done:
-            done.add(p)
+    waited = set()
+
+    def have_factors(p):
+        if p not in waited:
+            waited.add(p)
             factors_end(p)
 
-    def chain(part, at):
-        if at < 0 or at >= 3 * PER:
-            return
-        level, step = divmod(at, PER)
-        u = unit(level, part)
-        if step == 0:
+    def have_solved(u):
+        if ("s", u) not in waited:
+            waited.add(("s", u))
+            gather_end(u)
+
+    def step_of(kind, *at):
+        if kind == 0:
+            level, part = at
             if level > 0:
-                need(pair_of(level - 1, level))
+                if "rest" not in waited:
+                    waited.add("rest")
+                    for copy in loads[2:] + tables:
+                        copy.wait()
+                    for other in range(1, LEVELS):
+                        turn(other)
+                have_solved(unit(level - 1, part))
+                have_factors(pair_of(level - 1, level))
                 solve(level, part)
-            gather_start(u)
-        elif step <= 5:
-            gather_step(u, step - 1)
-            if step == 3 and level == 1:
-                need(pair_of(0, 2))
-                later(0, 2, part)
-            if step == 5 and level == 2:
-                need(pair_of(0, 3))
-                later(0, 3, part)
+            if level < LEVELS - 1:
+                gather_start(unit(level, part))
+        elif kind == 1:
+            gather_near(unit(*at))
+        elif kind == 2:
+            gather_ring(unit(at[0], at[1]), *at[2:])
+        elif kind == 3:
+            gather_last(unit(at[0], at[1]), at[2])
+        elif kind == 4:
+            lower, upper, part = at
+            have_solved(unit(lower, part))
+            have_factors(pair_of(lower, upper))
+            later(lower, upper, part)
         else:
-            gather_end(u)
-
-    for tick in range(3 * PER + LAG + 8):
-        for i, p in enumerate(PAIR_ORDER):
-            if tick == EVERY * i + SECOND:
-                factors_second(p)
-            if tick == EVERY * i + THIRD:
-                factors_third(p)
-        chain(0, tick)
-        for i, p in enumerate(PAIR_ORDER):
-            if tick == EVERY * i:
-                factors_send(p)
-        chain(1, tick - LAG)
-        if tick == 4:
-            for level in range(1, LEVELS):
-                turn(level)
-    need(pair_of(1, 3))
-    for part in range(PARTS):
-        later(1, 3, part)
-    for level in range(LEVELS - 1):
-        write(level)
-    need(pair_of(2, 3))
-    for part in range(PARTS):
-        solve(3, part)
-    write(3)
+            (factors_send, factors_far, factors_onward, factors_around, factors_last)[kind - 5](*at)
+
+    for step in STEPS:
+        if step[:2] == (0, LEVELS - 1) and "out" not in waited:
+            waited.add("out")
+            for level in range(LEVELS - 1):
+                write(level)
+        step_of(*step)
+    write(LEVELS - 1)
     for copy in sends:
         copy.wait_send()
 
 
 def per_device(right_side, diag_inverse, factors, pattern, owner_map):
     vmem = pl.BlockSpec(memory_space=pltpu.VMEM)
-    smem = pl.BlockSpec(memory_space=pltpu.SMEM)
+    anywhere = pl.BlockSpec(memory_space=pl.ANY)
     return pl.pallas_call(
         kernel,
         out_shape=jax.ShapeDtypeStruct(right_side.shape, jnp.bfloat16),
-        in_specs=[smem, smem, vmem, vmem, pl.BlockSpec(memory_space=pl.ANY)],
+        in_specs=[anywhere] * 5,
         out_specs=vmem,
         scratch_shapes=[pltpu.VMEM((SUPS, CHUNK, BLK), jnp.bfloat16)] * (3 * PARTS)
         + [
@@ -325,13 +356,18 @@
             pltpu.VMEM((LEVELS, PARTS, OWN, CHUNK, BLK), jnp.float32),
             pltpu.VMEM((LEVELS, OWN, COLS, BLK), jnp.bfloat16),
             pltpu.VMEM((OWN, COLS, BLK), jnp.bfloat16),
+            pltpu.SMEM(pattern.shape, jnp.int32),
+            pltpu.SMEM(owner_map.shape, jnp.int32),
+            pltpu.VMEM(right_side.shape, jnp.bfloat16),
+            pltpu.VMEM(diag_inverse.shape, jnp.bfloat16),
             pltpu.SemaphoreType.DMA((3 * PARTS, GATHER_SEMS)),
             pltpu.SemaphoreType.DMA((3 * PARTS, GATHER_SEMS)),
             pltpu.SemaphoreType.DMA((PAIRS, FACTOR_SEMS)),
             pltpu.SemaphoreType.DMA((PAIRS, FACTOR_SEMS)),
             pltpu.SemaphoreType.DMA((PAIRS,)),
+            pltpu.SemaphoreType.DMA((3, LEVELS)),
         ],
-        compiler_params=pltpu.CompilerParams(collective_id=0, has_side_effects=True, vmem_limit_bytes=48 << 20),
+        compiler_params=pltpu.CompilerParams(collective_id=0, has_side_effects=True, vmem_limit_bytes=62 << 20),
         name="substitution",
     )(pattern, owner_map, right_side, diag_inverse, factors)
 

time: 134 us -> 106 us (0.79)
  the two profiles are of different devices: /device:TPU:16 before, /device:TPU:1 now
where the time goes in v2:
time: 106 us
  Pallas kernels  104 us (98%)
  local copies, waits for them, and re-layouts  1.89 us (2%)
    pallas_call x1, Pallas kernels, per_device(): pl.pallas_call(kernel, out_shape=jax.ShapeDtypeStruct(right_side.shape, j...  104 us

profile of v2, /device:TPU:1, one launch (start us, length us, event | category | flops | bytes accessed | tf_op | source)
XLA Modules:
  0.0 106.1 jit_solution(9189753803926858749)
XLA Ops:
  0.0 104.2 %substitution.1 = bf16[4,4,128,128]{3,2,1,0:T(8,128)(2,1)} custom-call(s32[6,4,16]{2,1,0:T(4,128)} %refs_0_.1, s32[3,128]{1,0:T(4,128)} %refs_1_.1, bf16[4,4,128,128]{3,2,1,0:T(8,128)(2,1)} %refs_2_.1, bf16[4,4,128,128]{3,2,1,0:T(8,128)(2,1)} %refs_3_.1, bf16[6,4,2,128,128]{4,3,2,1,0:T(8,128)(2,1)} %refs_4_.1), custom_call_target="tpu_custom_call" | custom-call | tf_op jit(solution)/shard_map/substitution/pallas_call | solution.py:348
  104.2 1.9 %copy.7 = bf16[4,4,128,128]{3,2,1,0:T(8,128)(2,1)} copy(bf16[4,4,128,128]{3,2,1,0:T(8,128)(2,1)} %substitution.1) | data formatting | bytes 1048576

commit v3 on v2

--- a/solution.py
+++ b/solution.py
@@ -41,8 +41,10 @@
     (3,2,1,1), (4,1,3,1), (3,2,0,1), (3,2,0,0), (0,3,1), (0,3,0),
 )
 
-GATHER_SEMS = 33
-FACTOR_SEMS = 15
+GATHER_SEMS = 16
+LINE, SIDE = 13, 15
+FACTOR_SEM = {0: 0, 1: 1, 4: 2, 7: 3, 8: 4, 9: 5, 10: 5}
+FACTOR_END = 6
 MESH = pl.DeviceIdType.MESH
 
 
@@ -84,14 +86,11 @@
     y_down = (leaf, y_at(-1) * 2 + x_hi)
     partners = (z_up, z_down, x_near, sibling, x_far, y_up, y_down)
 
-    sends = []
-
     def send(src, dst, send_sem, recv_sem, device):
         copy = pltpu.make_async_remote_copy(
             src_ref=src, dst_ref=dst, send_sem=send_sem, recv_sem=recv_sem, device_id=device, device_id_type=MESH
         )
         copy.start()
-        sends.append(copy)
 
     def arrived(dst, recv_sem, send_sem):
         pltpu.make_async_remote_copy(
@@ -105,24 +104,21 @@
         return solved[u].at[pl.ds(first + half * (OWN // 2), OWN // 2)]
 
     def g_put(u, ref, at, device):
-        send(ref, ref, g_send.at[u, at], g_recv.at[u, at], device)
+        send(ref, ref, g_send.at[u], g_recv.at[u, at], device)
 
     def g_wait(u, ref, at):
-        arrived(ref, g_recv.at[u, at], g_send.at[u, at])
+        arrived(ref, g_recv.at[u, at], g_send.at[u])
 
     columns = (x_lo, 1 - x_lo)
 
     def ring(stream, down, step):
-        return 1 + stream * 8 + down * 4 + step - 1
-
-    def side(stream, offset):
-        return 17 + stream * 8 + offset % ZS
+        return LINE + stream if step == 4 else 1 + stream * 6 + down * 3 + step - 1
 
     def spread(u, stream):
         block = slots(u, columns[stream], z, core)
         g_put(u, block, ring(stream, 0, 1), z_up)
         g_put(u, block, ring(stream, 1, 1), z_down)
-        g_put(u, block, side(stream, 0), sibling)
+        g_put(u, block, SIDE, sibling)
 
     def gather_start(u):
         g_put(u, slots(u, x_lo, z, core), 0, x_near)
@@ -138,18 +134,22 @@
         g_wait(u, block, ring(stream, down, hop))
         onward = block if hop < 3 else slots(u, xl, z_at(offset), core, down)
         g_put(u, onward, ring(stream, down, hop + 1), z_down if down else z_up)
-        g_put(u, block, side(stream, offset), sibling)
+        g_put(u, block, SIDE, sibling)
 
     def gather_last(u, stream):
         xl = columns[stream]
-        for down in range(2):
-            g_wait(u, slots(u, xl, z_at(4), core, down), ring(stream, down, 4))
-        g_put(u, slots(u, xl, z_at(4), core), side(stream, 4), sibling)
+        g_wait(u, slots(u, xl, z_at(4), core), LINE + stream)
+        g_put(u, slots(u, xl, z_at(4), core), SIDE, sibling)
 
     def gather_end(u):
-        for stream in range(2):
-            for offset in range(ZS):
-                g_wait(u, slots(u, columns[stream], z_at(offset), 1 - core), side(stream, offset))
+        g_wait(u, solved[u].at[pl.ds(0, SUPS // 2)], SIDE)
+
+    def gather_sent(u):
+        ref = solved[u].at[pl.ds(0, OWN * (1 + 2 * (ZS - 1)) + SUPS // 2)]
+        pltpu.make_async_remote_copy(
+            src_ref=ref, dst_ref=ref, send_sem=g_send.at[u], recv_sem=g_recv.at[u, 0],
+            device_id=sibling, device_id_type=MESH,
+        ).wait_send()
 
     def held(p, yy, xh, y_first, half=None):
         cut = X_FIRST[p]
@@ -159,10 +159,10 @@
         return factors.at[p, yy * 2 + xh, which, pl.ds(half, 1)]
 
     def f_put(p, src, dst, at, device):
-        send(src, dst, f_send.at[p, at], f_recv.at[p, at], device)
+        send(src, dst, f_send.at[p], f_recv.at[p, FACTOR_SEM.get(at, FACTOR_END)], device)
 
     def f_wait(p, ref, at):
-        arrived(ref, f_recv.at[p, at], f_send.at[p, at])
+        arrived(ref, f_recv.at[p, FACTOR_SEM.get(at, FACTOR_END)], f_send.at[p])
 
     def own_copy(p):
         return pltpu.make_async_copy(own_factors.at[p], factors.at[p, launch], own_sem.at[p])
@@ -203,19 +203,20 @@
         f_put(p, block, block, 5 + down, y_down if down else y_up)
 
     def factors_last(p):
-        for half in range(2):
-            f_wait(p, held(p, y_at(2), x_hi, True, half), 9 + half)
         opposite = held(p, y_at(2), x_hi, True)
+        f_wait(p, opposite, 9)
         f_put(p, opposite, opposite, 14, x_far)
 
     def factors_end(p):
-        f_wait(p, held(p, y_at(1), x_hi, False), 2)
-        f_wait(p, held(p, y_at(-1), 1 - x_hi, False), 3)
-        f_wait(p, held(p, y_at(2), x_hi, False), 5)
-        f_wait(p, held(p, y_at(2), 1 - x_hi, False), 6)
-        for at, step in ((11, 0), (12, -1), (13, 1), (14, 2)):
-            f_wait(p, held(p, y_at(step), 1 - x_hi, True), at)
+        arrived(factors.at[p, pl.ds(0, 4)], f_recv.at[p, FACTOR_END], f_send.at[p])
         own_copy(p).wait()
+
+    def factors_sent(p):
+        ref = factors.at[p, pl.ds(0, 7)]
+        pltpu.make_async_remote_copy(
+            src_ref=ref, dst_ref=ref, send_sem=f_send.at[p], recv_sem=f_recv.at[p, 0],
+            device_id=sibling, device_id_type=MESH,
+        ).wait_send()
 
     def unit(level, part):
         return level * PARTS + part
@@ -273,8 +274,8 @@
     for device in partners:
         pl.semaphore_signal(barrier, inc=1, device_id=device, device_id_type=MESH)
     loads = [
-        pltpu.make_async_copy(src.at[part], dst.at[part], in_sem.at[at, part])
-        for part in range(LEVELS)
+        pltpu.make_async_copy(src.at[levels], dst.at[levels], in_sem.at[at, part])
+        for part, levels in enumerate((pl.ds(0, 1), pl.ds(1, LEVELS - 1)))
         for at, (src, dst) in enumerate(((right_side_in, right_side), (diag_in, diag)))
     ]
     tables = [
@@ -338,8 +339,10 @@
                 write(level)
         step_of(*step)
     write(LEVELS - 1)
-    for copy in sends:
-        copy.wait_send()
+    for u in range(3 * PARTS):
+        gather_sent(u)
+    for p in range(PAIRS):
+        factors_sent(p)
 
 
 def per_device(right_side, diag_inverse, factors, pattern, owner_map):
@@ -360,12 +363,12 @@
             pltpu.SMEM(owner_map.shape, jnp.int32),
             pltpu.VMEM(right_side.shape, jnp.bfloat16),
             pltpu.VMEM(diag_inverse.shape, jnp.bfloat16),
+            pltpu.SemaphoreType.DMA((3 * PARTS,)),
             pltpu.SemaphoreType.DMA((3 * PARTS, GATHER_SEMS)),
-            pltpu.SemaphoreType.DMA((3 * PARTS, GATHER_SEMS)),
-            pltpu.SemaphoreType.DMA((PAIRS, FACTOR_SEMS)),
-            pltpu.SemaphoreType.DMA((PAIRS, FACTOR_SEMS)),
             pltpu.SemaphoreType.DMA((PAIRS,)),
-            pltpu.SemaphoreType.DMA((3, LEVELS)),
+            pltpu.SemaphoreType.DMA((PAIRS, FACTOR_END + 1)),
+            pltpu.SemaphoreType.DMA((PAIRS,)),
+            pltpu.SemaphoreType.DMA((3, 2)),
         ],
         compiler_params=pltpu.CompilerParams(collective_id=0, has_side_effects=True, vmem_limit_bytes=62 << 20),
         name="substitution",

time: 106 us -> 102 us (0.962)
  Pallas kernels: 104 us -> 99.8 us
    pallas_call x1, Pallas kernels: 104 us -> 99.8 us  [per_device(): pl.pallas_call(kernel, out_shape=jax.ShapeDtypeStruct(right_side.shape, j...]
where the time goes in v3:
time: 102 us
  Pallas kernels  99.8 us (98%)
  local copies, waits for them, and re-layouts  1.89 us (2%)
    pallas_call x1, Pallas kernels, per_device(): pl.pallas_call(kernel, out_shape=jax.ShapeDtypeStruct(right_side.shape, j...  99.8 us

profile of v3, /device:TPU:1, one launch (start us, length us, event | category | flops | bytes accessed | tf_op | source)
XLA Modules:
  0.0 101.7 jit_solution(13110302462148317646)
XLA Ops:
  0.0 99.8 %substitution.1 = bf16[4,4,128,128]{3,2,1,0:T(8,128)(2,1)} custom-call(s32[6,4,16]{2,1,0:T(4,128)} %refs_0_.1, s32[3,128]{1,0:T(4,128)} %refs_1_.1, bf16[4,4,128,128]{3,2,1,0:T(8,128)(2,1)} %refs_2_.1, bf16[4,4,128,128]{3,2,1,0:T(8,128)(2,1)} %refs_3_.1, bf16[6,4,2,128,128]{4,3,2,1,0:T(8,128)(2,1)} %refs_4_.1), custom_call_target="tpu_custom_call" | custom-call | tf_op jit(solution)/shard_map/substitution/pallas_call | solution.py:351
  99.8 1.9 %copy.7 = bf16[4,4,128,128]{3,2,1,0:T(8,128)(2,1)} copy(bf16[4,4,128,128]{3,2,1,0:T(8,128)(2,1)} %substitution.1) | data formatting | bytes 1048576

commit v4 on v3

--- a/solution.py
+++ b/solution.py
@@ -18,27 +18,27 @@
 YS = 4
 LEAFS = 16
 
-X_FIRST = (2, 2, 3, 3, 3, 2)
+X_FIRST = (3, 3, 2, 2, 2, 3)
 
 STEPS = (
-    (5,0,2), (0,0,0), (5,1,2), (0,0,1), (5,0,0), (5,3,2), (1,0,0), (5,0,1), (5,3,0), (7,0,1), (7,0,0), (2,0,1,0,0,1),
-    (2,0,0,0,1,1), (5,0,3), (2,0,0,0,0,1), (5,3,1), (2,0,0,1,0,1), (2,0,0,1,1,1), (1,0,1), (5,4,3), (2,0,1,0,1,1),
-    (2,0,0,0,0,2), (2,0,0,1,0,2), (2,0,1,1,0,1), (9,0), (6,0), (5,4,1), (2,0,0,1,1,2), (2,0,1,1,1,1), (2,0,0,0,1,2),
-    (2,0,1,0,1,2), (2,0,0,1,1,3), (8,0,0), (7,3,0), (2,0,0,0,0,3), (2,0,1,1,0,2), (8,0,1), (2,0,1,1,1,2),
-    (2,0,0,1,0,3), (5,1,1), (2,0,1,0,0,2), (5,2,0), (7,3,1), (2,0,0,0,1,3), (2,0,1,1,1,3), (2,0,1,1,0,3), (3,0,0,0),
-    (5,4,2), (2,0,1,0,0,3), (3,0,0,1), (6,3), (5,5,2), (5,2,2), (2,0,1,0,1,3), (0,1,0), (5,1,0), (3,0,1,1), (3,0,1,0),
-    (0,1,1), (2,1,0,0,0,1), (1,1,0), (2,1,0,0,1,1), (5,4,0), (7,1,1), (2,1,1,0,1,1), (1,1,1), (2,1,1,0,0,1), (5,5,1),
-    (2,1,0,1,0,1), (5,1,3), (6,1), (2,1,0,1,1,1), (7,1,0), (2,1,1,1,0,1), (8,3,1), (2,1,1,0,0,2), (2,1,1,1,1,1),
-    (2,1,0,0,1,2), (2,1,0,1,1,2), (8,3,0), (2,1,0,1,0,2), (9,3), (2,1,1,1,0,2), (2,1,1,0,1,2), (9,1), (8,1,1),
-    (2,1,0,0,0,2), (2,1,1,0,0,3), (7,4,0), (2,1,1,1,1,2), (5,3,3), (5,5,0), (8,1,0), (2,1,0,1,1,3), (2,1,0,0,1,3),
-    (6,2), (7,4,1), (2,1,0,1,0,3), (5,2,1), (2,1,1,1,0,3), (6,4), (2,1,0,0,0,3), (2,1,1,0,1,3), (3,1,0,1),
-    (2,1,1,1,1,3), (4,0,2,1), (3,1,0,0), (4,0,2,0), (3,1,1,0), (0,2,0), (5,2,3), (3,1,1,1), (0,2,1), (7,2,0), (1,2,0),
-    (7,5,0), (2,2,0,0,0,1), (2,2,0,0,1,1), (7,2,1), (6,5), (7,5,1), (8,2,1), (1,2,1), (2,2,1,0,0,1), (8,2,0),
-    (2,2,1,0,1,1), (9,4), (2,2,0,1,0,1), (8,4,1), (2,2,0,0,1,2), (2,2,1,1,0,1), (2,2,1,1,1,1), (2,2,0,1,1,1),
-    (2,2,1,0,0,2), (2,2,1,0,1,2), (9,2), (9,5), (2,2,0,1,0,2), (8,4,0), (2,2,1,1,0,2), (2,2,1,1,1,2), (5,5,3),
-    (2,2,0,0,0,2), (8,5,1), (2,2,0,1,1,2), (2,2,1,0,1,3), (2,2,1,0,0,3), (8,5,0), (4,0,3,0), (2,2,1,1,0,3),
-    (2,2,1,1,1,3), (2,2,0,0,1,3), (2,2,0,1,0,3), (4,0,3,1), (2,2,0,1,1,3), (2,2,0,0,0,3), (4,1,3,0), (3,2,1,0),
-    (3,2,1,1), (4,1,3,1), (3,2,0,1), (3,2,0,0), (0,3,1), (0,3,0),
+    (5,0,1), (0,0,0), (5,0,2), (0,0,1), (5,3,2), (5,0,0), (5,1,0), (5,3,0), (5,4,2), (1,0,0), (2,0,0,0,0,1),
+    (2,0,0,0,1,1), (1,0,1), (2,0,1,0,1,1), (5,1,2), (2,0,0,1,0,1), (2,0,0,1,1,1), (6,0), (2,0,0,0,0,2), (2,0,0,0,1,2),
+    (5,0,3), (7,0,1), (5,4,0), (2,0,1,1,0,1), (7,0,0), (2,0,1,0,0,1), (2,0,1,1,1,1), (7,1,0), (2,0,1,0,1,2),
+    (2,0,0,1,1,2), (2,0,0,1,0,2), (7,1,1), (8,0,0), (2,0,0,0,1,3), (2,0,0,0,0,3), (6,3), (2,0,1,1,0,2), (2,0,1,1,1,2),
+    (8,0,1), (5,1,1), (2,0,1,0,0,2), (9,0), (7,3,0), (2,0,0,1,0,3), (6,1), (2,0,0,1,1,3), (2,0,1,1,1,3),
+    (2,0,1,0,1,3), (2,0,1,1,0,3), (2,0,1,0,0,3), (7,4,0), (3,0,0,1), (3,0,0,0), (0,1,0), (3,0,1,1), (3,0,1,0),
+    (0,1,1), (7,3,1), (5,2,2), (9,1), (1,1,0), (1,1,1), (5,3,3), (2,1,1,0,1,1), (2,1,0,0,1,1), (5,3,1), (8,1,1),
+    (2,1,0,0,0,1), (2,1,1,0,0,1), (5,1,3), (5,5,0), (2,1,1,1,0,1), (2,1,1,1,1,1), (8,1,0), (5,4,1), (7,4,1), (9,3),
+    (5,2,0), (2,1,0,1,0,1), (2,1,0,1,1,1), (2,1,1,0,1,2), (8,3,0), (2,1,1,0,0,2), (2,1,1,1,0,2), (2,1,1,1,1,2),
+    (2,1,0,1,0,2), (2,1,0,0,1,2), (8,3,1), (5,5,1), (2,1,0,1,1,2), (2,1,0,0,0,2), (5,5,2), (2,1,1,0,0,3),
+    (2,1,1,0,1,3), (4,0,2,0), (2,1,1,1,1,3), (2,1,1,1,0,3), (2,1,0,0,1,3), (2,1,0,1,0,3), (2,1,0,0,0,3),
+    (2,1,0,1,1,3), (7,2,1), (5,2,1), (6,4), (3,1,1,0), (3,1,1,1), (4,0,2,1), (0,2,1), (3,1,0,0), (8,4,0), (3,1,0,1),
+    (0,2,0), (9,4), (6,5), (1,2,1), (2,2,1,0,0,1), (5,4,3), (2,2,1,0,1,1), (1,2,0), (2,2,0,0,0,1), (7,5,0),
+    (2,2,0,0,1,1), (7,2,0), (6,2), (2,2,1,1,0,1), (8,4,1), (2,2,1,1,1,1), (8,2,0), (7,5,1), (2,2,0,1,0,1),
+    (2,2,0,1,1,1), (2,2,1,0,1,2), (2,2,0,0,0,2), (2,2,1,1,0,2), (2,2,1,1,1,2), (2,2,0,0,1,2), (5,2,3), (2,2,0,1,0,2),
+    (8,2,1), (2,2,0,1,1,2), (9,2), (2,2,1,0,0,2), (2,2,0,0,0,3), (8,5,1), (2,2,1,0,1,3), (8,5,0), (4,1,3,1), (5,5,3),
+    (2,2,1,1,1,3), (9,5), (2,2,1,1,0,3), (2,2,0,0,1,3), (4,1,3,0), (2,2,0,1,0,3), (2,2,0,1,1,3), (2,2,1,0,0,3),
+    (3,2,0,0), (4,0,3,0), (3,2,1,1), (3,2,0,1), (4,0,3,1), (3,2,1,0), (0,3,0), (0,3,1),
 )
 
 GATHER_SEMS = 16
@@ -230,10 +230,15 @@
             total += transposed_product(jnp.concatenate(picked, axis=1), jnp.concatenate(blocks, axis=1))
         return total
 
+    started = set()
+
     def later(lower, upper, part):
+        first = (upper, part) not in started
+        started.add((upper, part))
+
         def body(a, _):
             product = update(lower, upper, part, a)
-            if lower > 0:
+            if not first:
                 product += pending[upper, part, a]
             pending[upper, part, a] = product
             return 0

time: 102 us -> 101 us (level)
  no operation moved by 1% of the time
where the time goes in v4:
time: 101 us
  Pallas kernels  99.2 us (98%)
  local copies, waits for them, and re-layouts  1.89 us (2%)
    pallas_call x1, Pallas kernels, per_device(): pl.pallas_call(kernel, out_shape=jax.ShapeDtypeStruct(right_side.shape, j...  99.2 us

profile of v4, /device:TPU:1, one launch (start us, length us, event | category | flops | bytes accessed | tf_op | source)
XLA Modules:
  0.0 101.1 jit_solution(2429905061896404740)
XLA Ops:
  0.0 99.2 %substitution.1 = bf16[4,4,128,128]{3,2,1,0:T(8,128)(2,1)} custom-call(s32[6,4,16]{2,1,0:T(4,128)} %refs_0_.1, s32[3,128]{1,0:T(4,128)} %refs_1_.1, bf16[4,4,128,128]{3,2,1,0:T(8,128)(2,1)} %refs_2_.1, bf16[4,4,128,128]{3,2,1,0:T(8,128)(2,1)} %refs_3_.1, bf16[6,4,2,128,128]{4,3,2,1,0:T(8,128)(2,1)} %refs_4_.1), custom_call_target="tpu_custom_call" | custom-call | tf_op jit(solution)/shard_map/substitution/pallas_call | solution.py:356
  99.2 1.9 %copy.7 = bf16[4,4,128,128]{3,2,1,0:T(8,128)(2,1)} copy(bf16[4,4,128,128]{3,2,1,0:T(8,128)(2,1)} %substitution.1) | data formatting | bytes 1048576
